TPU v7x, 256 devices: a whole 4x4x8 slice. The times are simulated.
256 devices in a mesh: row: 16 (over y, z_lo, core), col: 16 (over z_hi, x).
Axes of the slice: x: 4, y: 4, z: 8 (z_hi: 4, z_lo: 2; z = z_hi * 2 + z_lo), core: 2. Of those that a mesh axis runs over, the one named last changes fastest.
Arguments:
- layer_input: bfloat16 [2048, 12288], P('col', 'row'), may hold values from -6 to 6
- out_grad: bfloat16 [2048, 12288], P('col', 'row'), may hold values from -6 to 6
- preact: bfloat16 [2048, 16384], P('row', 'col'), may hold values from -6 to 6
- weight_in: bfloat16 [12288, 16384], P('row', 'col'), may hold values from -0.0546875 to 0.0546875
- weight_out: bfloat16 [16384, 12288], P('col', 'row'), may hold values from -0.046875 to 0.046875
Outputs:
- input_grad: bfloat16 [2048, 12288], P('col', 'row')
- weight_in_grad: float32 [12288, 16384], P('row', 'col')
- weight_out_grad: float32 [16384, 12288], P('col', 'row')
All inputs are finite; a program needn't handle non-finite values.
Results may differ from a plain program's by a relative error of at most 0.019.
Values may be sent and summed in bfloat16 or wider, within the bound.
No kernel may reach another device: no remote copies, remote signals or barrier semaphores. Data moves between devices by JAX's collectives and lax.ppermute only.
A program may use at most 128 MiB of HBM per device.

v0:
```python
import math

import jax
import jax.numpy as jnp
from jax import lax
from jax.sharding import PartitionSpec as P


def gelu_parts(h):
    c = math.sqrt(2.0 / math.pi)
    t = jnp.tanh(c * (h + 0.044715 * h * h * h))
    value = 0.5 * h * (1.0 + t)
    slope = 0.5 * (1.0 + t) + 0.5 * h * (1.0 - t * t) * c * (1.0 + 3.0 * 0.044715 * h * h)
    return (value, slope)


def token_contract(left, right):
    return lax.dot_general(
        left, right, (((0,), (0,)), ((), ())), preferred_element_type=jnp.float32
    )


def width_contract(left, right):
    return lax.dot_general(
        left, right, (((1,), (1,)), ((), ())), preferred_element_type=jnp.float32
    )


def local(layer_input, out_grad, preact, weight_in, weight_out):
    input_panel, outgrad_panel = (
        lax.all_gather(layer_input, "col", axis=0, tiled=True),
        lax.all_gather(out_grad, "col", axis=0, tiled=True),
    )
    preact_full = lax.all_gather(preact, "row", axis=0, tiled=True)
    value, slope = gelu_parts(preact_full.astype(jnp.float32))
    activ_panel = value.astype(jnp.bfloat16)
    weight_out_grad = token_contract(activ_panel, outgrad_panel)
    tile_rows = preact.shape[0]
    part = outgrad_panel
    grad_act = lax.psum_scatter(
        width_contract(part, weight_out), "row", scatter_dimension=0, tiled=True
    )
    own_slope = lax.dynamic_slice_in_dim(slope, lax.axis_index("row") * tile_rows, tile_rows, 0)
    grad_pre = (grad_act * own_slope).astype(jnp.bfloat16)
    gradpre_panel = lax.all_gather(grad_pre, "row", axis=0, tiled=True)
    weight_in_grad = token_contract(input_panel, gradpre_panel)
    part = gradpre_panel
    input_grad = lax.psum_scatter(
        width_contract(part, weight_in).astype(jnp.bfloat16), "col", scatter_dimension=0, tiled=True
    )
    return (input_grad, weight_in_grad, weight_out_grad)


def solution(mesh):
    placed = (P("col", "row"), P("col", "row"), P("row", "col"), P("row", "col"), P("col", "row"))
    return jax.shard_map(
        local,
        mesh=mesh,
        in_specs=placed,
        out_specs=(P("col", "row"), P("row", "col"), P("col", "row")),
        check_vma=False,
    )
```

profile of v0, /device:TPU:1, one launch (start us, length us, event | category | flops | bytes accessed | tf_op | source)
XLA Modules:
  0.0 435.9 jit_solution(7078516410883646159)
XLA Ops:
  7.2 0.0 copy-start
  7.2 0.0 all-gather.5.cloned.1.call-start
  7.2 0.7 all-gather.5.cloned.1.call-update
  7.9 0.0 all-gather.7.cloned.1.call-start
  8.0 0.7 all-gather.7.cloned.1.call-update
  8.7 0.0 reduce-scatter.3.cloned.1.call-start
  8.7 73.2 %all-gather.5.cloned.1.call-done = bf16[2048,768]{1,0:T(8,128)(2,1)} async-done(((bf16[128,768]{1,0:T(8,128)(2,1)}), bf16[2048,768]{1,0:T(8,128)(2,1)}) %all-gather.5.cloned.1.call-update) | async-done | bytes 3145744 | tf_op jit(solution)/shard_map/all_gather | solution.py:32
  81.9 0.0 copy-done
  81.9 7.7 %fusion.12 = f32[2048,1024]{1,0:T(8,128)} fusion(bf16[2048,768]{1,0:T(8,128)(2,1)} %all-gather.5.cloned.1.call-done, bf16[1024,768]{1,0:T(8,128)(2,1)S(1)} %copy-done), kind=kOutput, calls=%fused_computation.21 | convolution fusion | flops 3221225472 | bytes 13107200 | tf_op jit(solution)/shard_map/dot_general | solution.py:24
  89.5 0.0 reduce-scatter.3.cloned.1.call-update
  89.6 0.0 all-gather.9.cloned.1.call-start
  89.6 32.6 %all-gather.7.cloned.1.call-done = bf16[2048,1024]{1,0:T(8,128)(2,1)} async-done(((bf16[128,1024]{1,0:T(8,128)(2,1)}), bf16[2048,1024]{1,0:T(8,128)(2,1)}) %all-gather.7.cloned.1.call-update) | async-done | bytes 4194320 | tf_op jit(solution)/shard_map/all_gather | solution.py:34
  122.3 0.0 copy-start.2
  122.3 6.6 %convert_element_type.12 = f32[2048,1024]{1,0:T(8,128)} convert(bf16[2048,1024]{1,0:T(8,128)(2,1)} %all-gather.7.cloned.1.call-done) | non-fusion elementwise | flops 2097152 | bytes 12582912 | tf_op jit(solution)/shard_map/convert_element_type | solution.py:35
  128.9 0.0 copy-done.2
  128.9 0.0 copy-start.3
  128.9 10.0 %fusion.1 = (f32[2048,1024]{1,0:T(8,128)}, f32[2048,1024]{1,0:T(8,128)}, f32[2048,1024]{1,0:T(8,128)}) fusion(bf16[2048,1024]{1,0:T(8,128)(2,1)S(1)} %copy-done.2), kind=kLoop, calls=%fused_computation.2 | loop fusion | flops 16777216 | bytes 29360128 | tf_op jit(solution)/shard_map/tanh | solution.py:11
  138.9 84.3 %reduce-scatter.3.cloned.1.call-done = f32[128,1024]{1,0:T(8,128)} async-done(((f32[2048,1024]{1,0:T(8,128)}), f32[128,1024]{1,0:T(8,128)}) %reduce-scatter.3.cloned.1.call-update) | async-done | bytes 524304 | tf_op jit(solution)/shard_map/reduce_scatter | solution.py:40
  223.2 2.6 fusion.7
  225.8 0.0 all-gather.9.cloned.1.call-update
  225.9 0.0 all-gather.11.cloned.1.call-start
  225.9 0.5 all-gather.11.cloned.1.call-update
  226.4 0.2 reduce-scatter.5.cloned.1.call-start
  226.7 39.8 %all-gather.9.cloned.1.call-done = bf16[2048,1024]{1,0:T(8,128)(2,1)} async-done(((bf16[128,1024]{1,0:T(8,128)(2,1)}), bf16[2048,1024]{1,0:T(8,128)(2,1)}) %all-gather.9.cloned.1.call-update) | async-done | bytes 4194320 | tf_op jit(solution)/shard_map/all_gather | solution.py:45
  266.5 0.0 copy-done.3
  266.5 7.4 %convolution_convert_fusion = bf16[2048,768]{1,0:T(8,128)(2,1)} fusion(bf16[2048,1024]{1,0:T(8,128)(2,1)} %all-gather.9.cloned.1.call-done, bf16[768,1024]{1,0:T(8,128)(2,1)S(1)} %copy-done.3), kind=kOutput, calls=%fused_computation.7 | convolution fusion | flops 3222798336 | bytes 8912896 | tf_op jit(solution)/shard_map/dot_general | solution.py:24
  273.9 0.0 reduce-scatter.5.cloned.1.call-update
  273.9 9.6 %fusion.2 = f32[1024,768]{1,0:T(8,128)} fusion(bf16[2048,768]{1,0:T(8,128)(2,1)} %all-gather.5.cloned.1.call-done, bf16[2048,1024]{1,0:T(8,128)(2,1)} %all-gather.7.cloned.1.call-done), kind=kOutput, calls=%fused_computation.4 | convolution fusion | flops 3242196992 | bytes 10485760 | tf_op jit(solution)/shard_map/dot_general | solution.py:18
  283.5 52.5 %all-gather.11.cloned.1.call-done = bf16[2048,768]{1,0:T(8,128)(2,1)} async-done(((bf16[128,768]{1,0:T(8,128)(2,1)}), bf16[2048,768]{1,0:T(8,128)(2,1)}) %all-gather.11.cloned.1.call-update) | async-done | bytes 3145744 | tf_op jit(solution)/shard_map/all_gather | solution.py:31
  336.0 0.0 copy-start.1
  336.0 8.5 %convolution_bitcast_fusion = f32[768,1024]{0,1:T(8,128)} fusion(bf16[2048,1024]{1,0:T(8,128)(2,1)} %all-gather.9.cloned.1.call-done, bf16[2048,768]{1,0:T(8,128)(2,1)} %all-gather.11.cloned.1.call-done), kind=kOutput, calls=%fused_computation.8 | convolution fusion | flops 3221225472 | bytes 10485760 | tf_op jit(solution)/shard_map/dot_general | solution.py:18
  344.5 3.5 copy.8
  348.1 80.9 %reduce-scatter.5.cloned.1.call-done = bf16[128,768]{1,0:T(8,128)(2,1)} async-done(((bf16[2048,768]{1,0:T(8,128)(2,1)}), bf16[128,768]{1,0:T(8,128)(2,1)}) %reduce-scatter.5.cloned.1.call-update) | async-done | bytes 196624 | tf_op jit(solution)/shard_map/reduce_scatter | solution.py:48
  429.0 0.0 copy-done.1
Async XLA Ops:
  7.2 74.7 %copy-start = (bf16[1024,768]{1,0:T(8,128)(2,1)S(1)}, bf16[1024,768]{1,0:T(8,128)(2,1)}, u32[]{:S(2)}) copy-start(bf16[1024,768]{1,0:T(8,128)(2,1)} %param.9) | copy-start | bytes 4718596
  7.2 74.7 %all-gather.5.cloned.1.call-start = ((), (), s32[]{:S(2)}) async-start(), calls=%async_computation.2 | async-start | bytes 3342336 | tf_op jit(solution)/shard_map/all_gather | solution.py:32
  7.9 114.3 %all-gather.7.cloned.1.call-start = ((), (), s32[]{:S(2)}) async-start(), calls=%async_computation.4 | async-start | bytes 4456448 | tf_op jit(solution)/shard_map/all_gather | solution.py:34
  8.7 214.5 %reduce-scatter.3.cloned.1.call-start = ((), (), s32[]{:S(2)}) async-start(), calls=%async_computation.3 | async-start | bytes 8912896 | tf_op jit(solution)/shard_map/reduce_scatter | solution.py:40
  89.6 176.9 %all-gather.9.cloned.1.call-start = ((), (), s32[]{:S(2)}) async-start(), calls=%async_computation.5 | async-start | bytes 4456448 | tf_op jit(solution)/shard_map/all_gather | solution.py:45
  122.3 6.6 %copy-start.2 = (bf16[2048,1024]{1,0:T(8,128)(2,1)S(1)}, bf16[2048,1024]{1,0:T(8,128)(2,1)}, u32[]{:S(2)}) copy-start(bf16[2048,1024]{1,0:T(8,128)(2,1)} %all-gather.7.cloned.1.call-done) | copy-start | bytes 12582916
  128.9 137.6 %copy-start.3 = (bf16[768,1024]{1,0:T(8,128)(2,1)S(1)}, bf16[768,1024]{1,0:T(8,128)(2,1)}, u32[]{:S(2)}) copy-start(bf16[768,1024]{1,0:T(8,128)(2,1)} %param.8) | copy-start | bytes 4718596
  225.9 110.1 %all-gather.11.cloned.1.call-start = ((), (), s32[]{:S(2)}) async-start(), calls=%async_computation.7 | async-start | bytes 3342336 | tf_op jit(solution)/shard_map/all_gather | solution.py:31
  226.4 202.6 %reduce-scatter.5.cloned.1.call-start = ((), (), s32[]{:S(2)}) async-start(), calls=%async_computation.6 | async-start | bytes 3342336 | tf_op jit(solution)/shard_map/reduce_scatter | solution.py:48
  336.0 93.0 %copy-start.1 = (bf16[1024,768]{1,0:T(8,128)(2,1)S(1)}, bf16[1024,768]{1,0:T(8,128)(2,1)}, u32[]{:S(2)}) copy-start(bf16[1024,768]{1,0:T(8,128)(2,1)} %param.9) | copy-start | bytes 4718596
Sparse Core Ops, SparseCore 0:
  10.4 71.3 all-gather.4
  83.7 38.4 all-gather.6
  124.8 98.3 reduce-scatter.2
  226.0 40.4 all-gather.8
  268.8 67.1 all-gather.10
  340.1 88.9 reduce-scatter.4
where the time goes:
time: 436 us
  waiting for transfers between devices  365 us (84%)
  matrix products  33.2 us (8%)
  other arithmetic  19.3 us (4%)
  between operations  14.1 us (3%)
    reduce_scatter x1, waiting for transfers between devices, local(): lax.psum_scatter(width_contract(part, weight_out), 'row', scatter_dimensi...  84.3 us
    reduce_scatter x1, waiting for transfers between devices, local(): lax.psum_scatter(width_contract(part, weight_in).astype(jnp.bfloat16), 'c...  80.9 us
    all_gather x1, waiting for transfers between devices, local(): lax.all_gather(out_grad, 'col', axis=0, tiled=True)  73.2 us
    all_gather x1, waiting for transfers between devices, local(): lax.all_gather(layer_input, 'col', axis=0, tiled=True)  52.5 us
    all_gather x1, waiting for transfers between devices, local(): gradpre_panel = lax.all_gather(grad_pre, 'row', axis=0, tiled=True)  39.8 us
    all_gather x1, waiting for transfers between devices, local(): preact_full = lax.all_gather(preact, 'row', axis=0, tiled=True)  32.6 us
    dot_general x2, matrix products, token_contract(): lax.dot_general(left, right, (((0,), (0,)), ((), ())), preferred_element_...  18.1 us
    dot_general x2, matrix products, width_contract(): lax.dot_general(left, right, (((1,), (1,)), ((), ())), preferred_element_...  15 us
  transfers between devices with their start and end apart: 6, of which 6 were waited for; matrix products, arithmetic and copies ran while one was open for 12% of the time, Pallas kernels for 0%

commit v1 on v0

v1 whole, which is shorter than its diff:
```python
import math

import jax
import jax.numpy as jnp
from jax import lax
from jax.sharding import PartitionSpec as P

BF = jnp.bfloat16
F32 = jnp.float32


def gelu_parts(h):
    c = math.sqrt(2.0 / math.pi)
    t = jnp.tanh(c * (h + 0.044715 * h * h * h))
    value = 0.5 * h * (1.0 + t)
    slope = 0.5 * (1.0 + t) + 0.5 * h * (1.0 - t * t) * c * (1.0 + 3.0 * 0.044715 * h * h)
    return (value, slope)


def token_contract(left, right):
    return lax.dot_general(left, right, (((0,), (0,)), ((), ())), preferred_element_type=F32)


def width_contract(left, right):
    return lax.dot_general(left, right, (((1,), (1,)), ((), ())), preferred_element_type=F32)


def move(v, axis, span, stride, step):
    def to(i):
        at = (i // stride) % span
        return i + (((at + step) % span) - at) * stride

    return lax.ppermute(v, axis, [(i, to(i)) for i in range(16)])


def along_x(v, d):
    return move(v, "col", 4, 1, d)


def along_zh(v, d):
    return move(v, "col", 4, 4, d)


def along_y(v, d):
    return move(v, "row", 4, 4, d)


def along_zl(v):
    return move(v, "row", 2, 2, 1)


def along_core(v):
    return move(v, "row", 2, 1, 1)


STEPS = (1, -1, 2)


def put(whole, piece, at, dim):
    return lax.dynamic_update_slice_in_dim(whole, jnp.expand_dims(piece, dim), at, dim)


def take(whole, at, dim):
    return lax.dynamic_index_in_dim(whole, at, dim, keepdims=False)


def gather4(shift, own, me, dim):
    shape = list(own.shape)
    shape.insert(dim, 4)
    whole = put(jnp.zeros(shape, own.dtype), own, me, dim)
    got = [(d, shift(own, d)) for d in STEPS]
    for d, piece in got:
        whole = put(whole, piece, (me - d) % 4, dim)
    return whole


def scatter4(shift, whole, me, dim):
    got = [shift(take(whole, (me + d) % 4, dim).astype(BF), d) for d in STEPS]
    total = take(whole, me, dim)
    for piece in got:
        total = total + piece.astype(F32)
    return total


def local(layer_input, out_grad, preact, weight_in, weight_out):
    col, row = lax.axis_index("col"), lax.axis_index("row")
    zh, x = col // 4, col % 4
    y, zl, core = row // 4, (row // 2) % 2, row % 2
    rows, width = out_grad.shape
    hidden = preact.shape[1]

    activ, slope = gelu_parts(preact.astype(F32))
    activ_panel = lax.all_gather(activ.astype(BF), "row", axis=0, tiled=True)
    input_panel = lax.all_gather(layer_input, "col", axis=0, tiled=True)

    by_z = gather4(along_zh, out_grad, zh, 0)
    og = gather4(along_x, by_z, x, 1)
    og_panel = og.reshape(16 * rows, width)
    og5 = og.reshape(4, 2, 2, rows, width)

    def grad_for(c):
        part = take(og5, c, 2).reshape(8 * rows, width)
        return width_contract(part, weight_out)

    away = along_core(grad_for(1 - core).astype(BF))
    mine = grad_for(core) + away.astype(F32)
    mine = mine.reshape(4, 2, rows, hidden)
    pair = scatter4(along_y, mine, y, 0)
    grad_act = take(pair, zl, 0) + along_zl(take(pair, 1 - zl, 0).astype(BF)).astype(F32)
    grad_pre = (grad_act * slope).astype(BF)

    other = along_zl(grad_pre)
    pair = put(put(jnp.zeros((2, rows, hidden), BF), grad_pre, zl, 0), other, 1 - zl, 0)
    half = gather4(along_y, pair, y, 0)
    rest = along_core(half)
    gp = put(put(jnp.zeros((4, 2, 2, rows, hidden), BF), half, core, 2), rest, 1 - core, 2)
    gp_panel = gp.reshape(16 * rows, hidden)

    partial = width_contract(gp_panel, weight_in).reshape(4, 4, rows, width)
    by_x = scatter4(along_x, partial, x, 1)
    input_grad = scatter4(along_zh, by_x, zh, 0).astype(BF)

    weight_out_grad = token_contract(activ_panel, og_panel)
    weight_in_grad = token_contract(input_panel, gp_panel)
    return (input_grad, weight_in_grad, weight_out_grad)


def solution(mesh):
    placed = (P("col", "row"), P("col", "row"), P("row", "col"), P("row", "col"), P("col", "row"))
    return jax.shard_map(
        local,
        mesh=mesh,
        in_specs=placed,
        out_specs=(P("col", "row"), P("row", "col"), P("col", "row")),
        check_vma=False,
    )
```

time: 436 us -> 270 us (0.62); the launches traced: 436 us -> 265 us
  waiting for transfers between devices: 365 us -> 148 us
  starting transfers between devices: 0.42 us -> 47.1 us
  local copies, waits for them, and re-layouts: 3.56 us -> 22.4 us
  other arithmetic: 19.3 us -> 5.55 us
  matrix products: 33.2 us -> 26.8 us
    all_gather x4 -> x2, waiting for transfers between devices: 198 us -> 0.01 us  [the longest x1 0.01 us: local(): input_panel = lax.all_gather(layer_input, 'col', axis=0, tiled=True)]
    reduce_scatter x2 -> x0, waiting for transfers between devices: 165 us -> none  [the longest x1 84.3 us: local(): lax.psum_scatter(width_contract(part, weight_out), 'row', scatter_dimensi...]
    ppermute x0 -> x22, waiting for transfers between devices: none -> 148 us  [move(): return lax.ppermute(v, axis, [(i, to(i)) for i in range(16)])]
    ppermute x0 -> x22, starting transfers between devices: none -> 47 us  [move(): return lax.ppermute(v, axis, [(i, to(i)) for i in range(16)])]
    tanh x1 -> x0, other arithmetic: 10 us -> none  [gelu_parts(): t = jnp.tanh(c * (h + 0.044715 * h * h * h))]
    dynamic_update_slice x0 -> x15, local copies, waits for them, and re-layouts: none -> 9.55 us  [put(): lax.dynamic_update_slice_in_dim(whole, jnp.expand_dims(piece, dim), at, dim)]
    convert_element_type x2, other arithmetic: 9.26 us -> 1.66 us  [the longest x1 0.89 us: local(): activ_panel = lax.all_gather(activ.astype(BF), 'row', axis=0, tiled=True)]
    dot_general x2 -> x3, matrix products: 15 us -> 10 us  [width_contract(): lax.dot_general(left, right, (((1,), (1,)), ((), ())), preferred_element_...]
  transfers between devices with their start and end apart: 6 -> 24, of which waited for: 6 -> 15; matrix products, arithmetic and copies ran while one was open for 12% -> 16% of each run, Pallas kernels for 0% -> 0%
where the time goes in v1:
time: 270 us; the launch traced here: 265 us
  waiting for transfers between devices  148 us (55%)
  starting transfers between devices  47.1 us (17%)
  matrix products  26.8 us (10%)
  local copies, waits for them, and re-layouts  22.4 us (8%)
  between operations  14.4 us (5%)
  other arithmetic  5.55 us (2%)
    ppermute x22, waiting for transfers between devices, move(): return lax.ppermute(v, axis, [(i, to(i)) for i in range(16)])  148 us
    ppermute x22, starting transfers between devices, move(): return lax.ppermute(v, axis, [(i, to(i)) for i in range(16)])  47 us
    dot_general x2, matrix products, token_contract(): lax.dot_general(left, right, (((0,), (0,)), ((), ())), preferred_element_...  16.8 us
    dot_general x3, matrix products, width_contract(): lax.dot_general(left, right, (((1,), (1,)), ((), ())), preferred_element_...  10 us
    dynamic_update_slice x15, local copies, waits for them, and re-layouts, put(): lax.dynamic_update_slice_in_dim(whole, jnp.expand_dims(piece, dim), at, dim)  9.55 us
    unnamed x17, local copies, waits for them, and re-layouts  8.36 us
  transfers between devices with their start and end apart: 24, of which 15 were waited for; matrix products, arithmetic and copies ran while one was open for 16% of the time, Pallas kernels for 0%

profile of v1, /device:TPU:1, one launch (start us, length us, event | category | flops | bytes accessed | tf_op | source)
XLA Modules:
  0.0 264.6 jit_solution(15261332621136797731)
XLA Ops:
  7.2 3.9 %collective-permute-start = (bf16[128,768]{1,0:T(8,128)(2,1)}, bf16[128,768]{1,0:T(8,128)(2,1)S(1)}, u32[]{:S(2)}, u32[]{:S(2)}) collective-permute-start(bf16[128,768]{1,0:T(8,128)(2,1)} %param.6), channel_id=1, source_target_pairs={{0,4},{1,5},{2,6},{3,7},{4,8},{5,9},{6,10},{7,11},{8,12},{9,13},{1... | collective-permute-start | bytes 589832 | tf_op jit(solution)/shard_map/ppermute | solution.py:33
  11.1 3.1 %collective-permute-start.1 = (bf16[128,768]{1,0:T(8,128)(2,1)}, bf16[128,768]{1,0:T(8,128)(2,1)S(1)}, u32[]{:S(2)}, u32[]{:S(2)}) collective-permute-start(bf16[128,768]{1,0:T(8,128)(2,1)} %param.6), channel_id=1, source_target_pairs={{0,12},{1,13},{2,14},{3,15},{4,0},{5,1},{6,2},{7,3},{8,4},{9,5},{1... | collective-permute-start | bytes 589832 | tf_op jit(solution)/shard_map/ppermute | solution.py:33
  14.2 4.4 %collective-permute-start.2 = (bf16[128,768]{1,0:T(8,128)(2,1)}, bf16[128,768]{1,0:T(8,128)(2,1)S(1)}, u32[]{:S(2)}, u32[]{:S(2)}) collective-permute-start(bf16[128,768]{1,0:T(8,128)(2,1)} %param.6), channel_id=1, source_target_pairs={{0,8},{1,9},{2,10},{3,11},{4,12},{5,13},{6,14},{7,15},{8,0},{9,1},... | collective-permute-start | bytes 589832 | tf_op jit(solution)/shard_map/ppermute | solution.py:33
  18.7 1.0 bitcast_dynamic-update-slice_fusion.15
  19.7 9.8 %collective-permute-done.1 = bf16[128,768]{1,0:T(8,128)(2,1)S(1)} collective-permute-done((bf16[128,768]{1,0:T(8,128)(2,1)}, bf16[128,768]{1,0:T(8,128)(2,1)S(1)}, u32[]{:S(2)}, u32[]{:S(2)}) %collective-permute-start.1) | collective-permute-done | bytes 196640 | tf_op jit(solution)/shard_map/ppermute | solution.py:33
  29.5 0.3 collective-permute-done.2
  29.8 1.3 collective-permute-start.3
  31.1 1.5 collective-permute-start.4
  32.7 1.6 collective-permute-start.5
  34.4 0.3 broadcast_in_dim.66
  34.7 13.2 %collective-permute-done.3 = bf16[4,128,768]{2,1,0:T(8,128)(2,1)} collective-permute-done((bf16[4,128,768]{2,1,0:T(8,128)(2,1)S(1)}, bf16[4,128,768]{2,1,0:T(8,128)(2,1)}, u32[]{:S(2)}, u32[]{:S(2)}) %collective-permute-start.3) | collective-permute-done | bytes 786464 | tf_op jit(solution)/shard_map/ppermute | solution.py:33
  47.9 1.2 bitcast_dynamic-update-slice_fusion.3
  49.2 19.6 %collective-permute-done.5 = bf16[4,128,768]{2,1,0:T(8,128)(2,1)S(1)} collective-permute-done((bf16[4,128,768]{2,1,0:T(8,128)(2,1)S(1)}, bf16[4,128,768]{2,1,0:T(8,128)(2,1)S(1)}, u32[]{:S(2)}, u32[]{:S(2)}) %collective-permute-start.5) | collective-permute-done | bytes 786464 | tf_op jit(solution)/shard_map/ppermute | solution.py:33
  68.9 0.3 constant_dynamic-slice_fusion
  69.2 1.3 copy-done.2
  70.5 3.1 %convolution_convert_fusion = bf16[1024,1024]{1,0:T(8,128)(2,1)} fusion(bf16[1024,768]{1,0:T(8,128)(2,1)S(1)} %bitcast.123, bf16[1024,768]{1,0:T(8,128)(2,1)S(1)} %copy-done), kind=kOutput, calls=%fused_computation.4 | convolution fusion | flops 1611661312 | bytes 5242880 | tf_op jit(solution)/shard_map/dot_general | solution.py:25
  73.7 3.3 %collective-permute-start.6 = (bf16[1024,1024]{1,0:T(8,128)(2,1)}, bf16[1024,1024]{1,0:T(8,128)(2,1)}, u32[]{:S(2)}, u32[]{:S(2)}) collective-permute-start(bf16[1024,1024]{1,0:T(8,128)(2,1)} %convolution_convert_fusion), channel_id=1, source_target_pairs={{0,16},{16,0},{32,48},{48,32},{64,80},{80,64},{96,112},{112,96},{1... | collective-permute-start | bytes 6291464 | tf_op jit(solution)/shard_map/ppermute | solution.py:33
  76.9 4.1 %collective-permute-done.6 = bf16[1024,1024]{1,0:T(8,128)(2,1)} collective-permute-done((bf16[1024,1024]{1,0:T(8,128)(2,1)}, bf16[1024,1024]{1,0:T(8,128)(2,1)}, u32[]{:S(2)}, u32[]{:S(2)}) %collective-permute-start.6) | collective-permute-done | bytes 2097184 | tf_op jit(solution)/shard_map/ppermute | solution.py:33
  81.0 3.4 %convert_add_fusion = f32[1024,1024]{1,0:T(8,128)S(1)} fusion(bf16[1024,1024]{1,0:T(8,128)(2,1)} %collective-permute-done.6, bf16[1024,768]{1,0:T(8,128)(2,1)S(1)} %bitcast.122, bf16[1024,768]{1,0:T(8,128)(2,1)S(1)} %copy-done), kind=kOutput, calls=%fused_computation | convolution fusion | flops 1612709888 | bytes 9437184 | tf_op jit(solution)/shard_map/dot_general | solution.py:25
  84.5 2.0 copy-done.5
  86.4 0.2 fusion.17
  86.7 1.4 collective-permute-start.7
  88.1 1.5 collective-permute-start.8
  89.6 1.6 collective-permute-start.9
  91.1 10.2 %collective-permute-done.7 = bf16[2,128,1024]{2,1,0:T(8,128)(2,1)S(1)} collective-permute-done((bf16[2,128,1024]{2,1,0:T(8,128)(2,1)S(1)}, bf16[2,128,1024]{2,1,0:T(8,128)(2,1)S(1)}, u32[]{:S(2)}, u32[]{:S(2)}) %collective-permute-start.7) | collective-permute-done | bytes 524320 | tf_op jit(solution)/shard_map/ppermute | solution.py:33
  101.3 12.3 %collective-permute-done.9 = bf16[2,128,1024]{2,1,0:T(8,128)(2,1)S(1)} collective-permute-done((bf16[2,128,1024]{2,1,0:T(8,128)(2,1)S(1)}, bf16[2,128,1024]{2,1,0:T(8,128)(2,1)S(1)}, u32[]{:S(2)}, u32[]{:S(2)}) %collective-permute-start.9) | collective-permute-done | bytes 524320 | tf_op jit(solution)/shard_map/ppermute | solution.py:33
  113.7 1.5 fusion.5
  115.3 6.6 %collective-permute-start.10 = (bf16[128,1024]{1,0:T(8,128)(2,1)S(1)}, bf16[128,1024]{1,0:T(8,128)(2,1)S(1)}, u32[]{:S(2)}, u32[]{:S(2)}) collective-permute-start(bf16[128,1024]{1,0:T(8,128)(2,1)S(1)} %fusion.26), channel_id=1, source_target_pairs={{0,32},{16,48},{32,0},{48,16},{64,96},{80,112},{96,64},{112,80},{1... | collective-permute-start | bytes 786440 | tf_op jit(solution)/shard_map/ppermute | solution.py:33
  121.8 0.9 fusion.16
  122.8 4.5 %collective-permute-done.10 = bf16[128,1024]{1,0:T(8,128)(2,1)S(1)} collective-permute-done((bf16[128,1024]{1,0:T(8,128)(2,1)S(1)}, bf16[128,1024]{1,0:T(8,128)(2,1)S(1)}, u32[]{:S(2)}, u32[]{:S(2)}) %collective-permute-start.10) | collective-permute-done | bytes 262176 | tf_op jit(solution)/shard_map/ppermute | solution.py:33
  127.3 0.4 bitcast_dynamic-update-slice_fusion.11
  127.7 1.3 collective-permute-start.11
  129.0 7.2 %collective-permute-done.11 = bf16[128,1024]{1,0:T(8,128)(2,1)S(1)} collective-permute-done((bf16[128,1024]{1,0:T(8,128)(2,1)S(1)}, bf16[128,1024]{1,0:T(8,128)(2,1)S(1)}, u32[]{:S(2)}, u32[]{:S(2)}) %collective-permute-start.11) | collective-permute-done | bytes 262176 | tf_op jit(solution)/shard_map/ppermute | solution.py:33
  136.2 0.1 collective-permute-start.12
  136.3 2.7 %collective-permute-start.13 = (bf16[2,128,1024]{2,1,0:T(8,128)(2,1)S(1)}, bf16[2,128,1024]{2,1,0:T(8,128)(2,1)S(1)}, u32[]{:S(2)}, u32[]{:S(2)}) collective-permute-start(bf16[2,128,1024]{2,1,0:T(8,128)(2,1)S(1)} %bitcast_dynamic-update-slice_fusion.10), channel_id=1, source_target_pairs={{0,192},{16,208},{32,224},{48,240},{64,0},{80,16},{96,32},{112,48}... | collective-permute-start | bytes 1572872 | tf_op jit(solution)/shard_map/ppermute | solution.py:33
  138.9 1.6 broadcast_in_dim.64
  140.5 0.8 bitcast_dynamic-update-slice_fusion.9
  141.3 15.8 %collective-permute-done.12 = bf16[2,128,1024]{2,1,0:T(8,128)(2,1)S(1)} collective-permute-done((bf16[2,128,1024]{2,1,0:T(8,128)(2,1)S(1)}, bf16[2,128,1024]{2,1,0:T(8,128)(2,1)S(1)}, u32[]{:S(2)}, u32[]{:S(2)}) %collective-permute-start.12) | collective-permute-done | bytes 524320 | tf_op jit(solution)/shard_map/ppermute | solution.py:33
  157.1 0.8 bitcast_dynamic-update-slice_fusion.8
  158.0 0.8 bitcast_dynamic-update-slice_fusion.7
  158.8 15.0 %collective-permute-done.14 = bf16[2,128,1024]{2,1,0:T(8,128)(2,1)S(1)} collective-permute-done((bf16[2,128,1024]{2,1,0:T(8,128)(2,1)S(1)}, bf16[2,128,1024]{2,1,0:T(8,128)(2,1)S(1)}, u32[]{:S(2)}, u32[]{:S(2)}) %collective-permute-start.14) | collective-permute-done | bytes 524320 | tf_op jit(solution)/shard_map/ppermute | solution.py:33
  173.8 0.8 bitcast_dynamic-update-slice_fusion.6
  174.6 3.2 %collective-permute-start.15 = (bf16[4,2,128,1024]{3,2,1,0:T(8,128)(2,1)}, bf16[4,2,128,1024]{3,2,1,0:T(8,128)(2,1)}, u32[]{:S(2)}, u32[]{:S(2)}) collective-permute-start(bf16[4,2,128,1024]{3,2,1,0:T(8,128)(2,1)} %bitcast_dynamic-update-slice_fusion.6), channel_id=1, source_target_pairs={{0,16},{16,0},{32,48},{48,32},{64,80},{80,64},{96,112},{112,96},{1... | collective-permute-start | bytes 6291464 | tf_op jit(solution)/shard_map/ppermute | solution.py:33
  177.8 0.5 broadcast_in_dim.63
  178.3 1.9 bitcast_dynamic-update-slice_fusion
  180.3 1.7 collective-permute-done.15
  181.9 1.9 bitcast_dynamic-update-slice_fusion.1
  183.9 3.5 %fusion = f32[4,4,128,768]{3,2,1,0:T(8,128)S(1)} fusion(bf16[4,4,128,1024]{3,2,1,0:T(8,128)(2,1)S(1)} %bitcast.118, bf16[768,1024]{1,0:T(8,128)(2,1)S(1)} %copy-done.7), kind=kOutput, calls=%fused_computation.7 | convolution fusion | flops 3221225472 | bytes 12058624 | tf_op jit(solution)/shard_map/dot_general | solution.py:25
  187.4 1.4 fusion.7
  188.8 1.5 copy-done.4
  190.3 1.2 collective-permute-start.16
  191.5 1.5 collective-permute-start.17
  192.9 1.1 collective-permute-start.18
  194.0 16.4 %collective-permute-done.16 = bf16[4,128,768]{2,1,0:T(8,128)(2,1)S(1)} collective-permute-done((bf16[4,128,768]{2,1,0:T(8,128)(2,1)}, bf16[4,128,768]{2,1,0:T(8,128)(2,1)S(1)}, u32[]{:S(2)}, u32[]{:S(2)}) %collective-permute-start.16) | collective-permute-done | bytes 786464 | tf_op jit(solution)/shard_map/ppermute | solution.py:33
  210.4 17.9 %collective-permute-done.18 = bf16[4,128,768]{2,1,0:T(8,128)(2,1)} collective-permute-done((bf16[4,128,768]{2,1,0:T(8,128)(2,1)S(1)}, bf16[4,128,768]{2,1,0:T(8,128)(2,1)}, u32[]{:S(2)}, u32[]{:S(2)}) %collective-permute-start.18) | collective-permute-done | bytes 786464 | tf_op jit(solution)/shard_map/ppermute | solution.py:33
  228.3 2.0 fusion.3
  230.4 0.1 collective-permute-start.19
  230.4 3.6 %collective-permute-start.20 = (bf16[128,768]{1,0:T(8,128)(2,1)S(1)}, bf16[128,768]{1,0:T(8,128)(2,1)S(1)}, u32[]{:S(2)}, u32[]{:S(2)}) collective-permute-start(bf16[128,768]{1,0:T(8,128)(2,1)S(1)} %get-tuple-element.24), channel_id=1, source_target_pairs={{0,12},{1,13},{2,14},{3,15},{4,0},{5,1},{6,2},{7,3},{8,4},{9,5},{1... | collective-permute-start | bytes 589832 | tf_op jit(solution)/shard_map/ppermute | solution.py:33
  234.0 2.4 collective-permute-start.21
  236.4 8.3 %convolution_bitcast_fusion = f32[768,1024]{0,1:T(8,128)} fusion(bf16[2048,1024]{1,0:T(8,128)(2,1)} %bitcast.119, bf16[2048,768]{1,0:T(8,128)(2,1)} %all-gather.3.cloned.1.call-done), kind=kOutput, calls=%fused_computation.3 | convolution fusion | flops 3221225472 | bytes 10485760 | tf_op jit(solution)/shard_map/dot_general | solution.py:21
  244.7 3.5 %copy.25 = f32[768,1024]{1,0:T(8,128)} copy(f32[768,1024]{0,1:T(8,128)} %convolution_bitcast_fusion) | data formatting | bytes 6291456
  248.3 0.3 collective-permute-done.21
  248.6 0.8 fusion.25
  249.3 8.4 %fusion.31 = f32[1024,768]{1,0:T(8,128)} fusion(bf16[2048,1024]{1,0:T(8,128)(2,1)} %all-gather.5.cloned.1.call-done, bf16[2048,768]{1,0:T(8,128)(2,1)} %bitcast.117), kind=kOutput, calls=%fused_computation.72 | convolution fusion | flops 3221225472 | bytes 10485760 | tf_op jit(solution)/shard_map/dot_general | solution.py:21
  (38 shorter events, 0.6 us)
Async XLA Ops:
  7.2 63.3 %copy-start = (bf16[1024,768]{1,0:T(8,128)(2,1)S(1)}, bf16[1024,768]{1,0:T(8,128)(2,1)}, u32[]{:S(2)}) copy-start(bf16[1024,768]{1,0:T(8,128)(2,1)} %param.9) | copy-start | bytes 4718596
  7.2 229.2 %all-gather.3.cloned.1.call-start = ((), (), s32[]{:S(2)}) async-start(), calls=%async_computation | async-start | bytes 3342336 | tf_op jit(solution)/shard_map/all_gather | solution.py:94
  7.2 12.4 %collective-permute-start = (bf16[128,768]{1,0:T(8,128)(2,1)}, bf16[128,768]{1,0:T(8,128)(2,1)S(1)}, u32[]{:S(2)}, u32[]{:S(2)}) collective-permute-start(bf16[128,768]{1,0:T(8,128)(2,1)} %param.6), channel_id=1, source_target_pairs={{0,4},{1,5},{2,6},{3,7},{4,8},{5,9},{6,10},{7,11},{8,12},{9,13},{1... | collective-permute-start | bytes 589832 | tf_op jit(solution)/shard_map/ppermute | solution.py:33
  11.1 18.4 %collective-permute-start.1 = (bf16[128,768]{1,0:T(8,128)(2,1)}, bf16[128,768]{1,0:T(8,128)(2,1)S(1)}, u32[]{:S(2)}, u32[]{:S(2)}) collective-permute-start(bf16[128,768]{1,0:T(8,128)(2,1)} %param.6), channel_id=1, source_target_pairs={{0,12},{1,13},{2,14},{3,15},{4,0},{5,1},{6,2},{7,3},{8,4},{9,5},{1... | collective-permute-start | bytes 589832 | tf_op jit(solution)/shard_map/ppermute | solution.py:33
  14.2 15.6 %collective-permute-start.2 = (bf16[128,768]{1,0:T(8,128)(2,1)}, bf16[128,768]{1,0:T(8,128)(2,1)S(1)}, u32[]{:S(2)}, u32[]{:S(2)}) collective-permute-start(bf16[128,768]{1,0:T(8,128)(2,1)} %param.6), channel_id=1, source_target_pairs={{0,8},{1,9},{2,10},{3,11},{4,12},{5,13},{6,14},{7,15},{8,0},{9,1},... | collective-permute-start | bytes 589832 | tf_op jit(solution)/shard_map/ppermute | solution.py:33
  29.8 18.1 %collective-permute-start.3 = (bf16[4,128,768]{2,1,0:T(8,128)(2,1)S(1)}, bf16[4,128,768]{2,1,0:T(8,128)(2,1)}, u32[]{:S(2)}, u32[]{:S(2)}) collective-permute-start(bf16[4,128,768]{2,1,0:T(8,128)(2,1)S(1)} %bitcast_dynamic-update-slice_fusion.12), channel_id=1, source_target_pairs={{0,1},{1,2},{2,3},{3,0},{4,5},{5,6},{6,7},{7,4},{8,9},{9,10},{10,1... | collective-permute-start | bytes 2359304 | tf_op jit(solution)/shard_map/ppermute | solution.py:33
  31.1 18.0 %collective-permute-start.4 = (bf16[4,128,768]{2,1,0:T(8,128)(2,1)S(1)}, bf16[4,128,768]{2,1,0:T(8,128)(2,1)S(1)}, u32[]{:S(2)}, u32[]{:S(2)}) collective-permute-start(bf16[4,128,768]{2,1,0:T(8,128)(2,1)S(1)} %bitcast_dynamic-update-slice_fusion.12), channel_id=1, source_target_pairs={{0,3},{1,0},{2,1},{3,2},{4,7},{5,4},{6,5},{7,6},{8,11},{9,8},{10,9... | collective-permute-start | bytes 2359304 | tf_op jit(solution)/shard_map/ppermute | solution.py:33
  32.6 216.7 %all-gather.5.cloned.1.call-start = ((), (), s32[]{:S(2)}) async-start(), calls=%async_computation.1 | async-start | bytes 4456448 | tf_op jit(solution)/shard_map/all_gather | solution.py:93
  32.7 36.1 %collective-permute-start.5 = (bf16[4,128,768]{2,1,0:T(8,128)(2,1)S(1)}, bf16[4,128,768]{2,1,0:T(8,128)(2,1)S(1)}, u32[]{:S(2)}, u32[]{:S(2)}) collective-permute-start(bf16[4,128,768]{2,1,0:T(8,128)(2,1)S(1)} %bitcast_dynamic-update-slice_fusion.12), channel_id=1, source_target_pairs={{0,2},{1,3},{2,0},{3,1},{4,6},{5,7},{6,4},{7,5},{8,10},{9,11},{10,... | collective-permute-start | bytes 2359304 | tf_op jit(solution)/shard_map/ppermute | solution.py:33
  68.9 1.6 copy-start.2
  73.7 7.4 %collective-permute-start.6 = (bf16[1024,1024]{1,0:T(8,128)(2,1)}, bf16[1024,1024]{1,0:T(8,128)(2,1)}, u32[]{:S(2)}, u32[]{:S(2)}) collective-permute-start(bf16[1024,1024]{1,0:T(8,128)(2,1)} %convolution_convert_fusion), channel_id=1, source_target_pairs={{0,16},{16,0},{32,48},{48,32},{64,80},{80,64},{96,112},{112,96},{1... | collective-permute-start | bytes 6291464 | tf_op jit(solution)/shard_map/ppermute | solution.py:33
  84.5 2.0 copy-start.5
  86.4 35.4 %copy-start.6 = (bf16[128,1024]{1,0:T(8,128)(2,1)S(1)}, bf16[128,1024]{1,0:T(8,128)(2,1)}, u32[]{:S(2)}) copy-start(bf16[128,1024]{1,0:T(8,128)(2,1)} %param.7) | copy-start | bytes 786436
  86.7 14.6 %collective-permute-start.7 = (bf16[2,128,1024]{2,1,0:T(8,128)(2,1)S(1)}, bf16[2,128,1024]{2,1,0:T(8,128)(2,1)S(1)}, u32[]{:S(2)}, u32[]{:S(2)}) collective-permute-start(bf16[2,128,1024]{2,1,0:T(8,128)(2,1)S(1)} %get-tuple-element.17), channel_id=1, source_target_pairs={{0,64},{16,80},{32,96},{48,112},{64,128},{80,144},{96,160},{112,17... | collective-permute-start | bytes 1572872 | tf_op jit(solution)/shard_map/ppermute | solution.py:33
  88.1 13.3 %collective-permute-start.8 = (bf16[2,128,1024]{2,1,0:T(8,128)(2,1)S(1)}, bf16[2,128,1024]{2,1,0:T(8,128)(2,1)S(1)}, u32[]{:S(2)}, u32[]{:S(2)}) collective-permute-start(bf16[2,128,1024]{2,1,0:T(8,128)(2,1)S(1)} %get-tuple-element.19), channel_id=1, source_target_pairs={{0,192},{16,208},{32,224},{48,240},{64,0},{80,16},{96,32},{112,48}... | collective-permute-start | bytes 1572872 | tf_op jit(solution)/shard_map/ppermute | solution.py:33
  89.6 24.1 %collective-permute-start.9 = (bf16[2,128,1024]{2,1,0:T(8,128)(2,1)S(1)}, bf16[2,128,1024]{2,1,0:T(8,128)(2,1)S(1)}, u32[]{:S(2)}, u32[]{:S(2)}) collective-permute-start(bf16[2,128,1024]{2,1,0:T(8,128)(2,1)S(1)} %get-tuple-element.18), channel_id=1, source_target_pairs={{0,128},{16,144},{32,160},{48,176},{64,192},{80,208},{96,224},{112... | collective-permute-start | bytes 1572872 | tf_op jit(solution)/shard_map/ppermute | solution.py:33
  115.3 12.0 %collective-permute-start.10 = (bf16[128,1024]{1,0:T(8,128)(2,1)S(1)}, bf16[128,1024]{1,0:T(8,128)(2,1)S(1)}, u32[]{:S(2)}, u32[]{:S(2)}) collective-permute-start(bf16[128,1024]{1,0:T(8,128)(2,1)S(1)} %fusion.26), channel_id=1, source_target_pairs={{0,32},{16,48},{32,0},{48,16},{64,96},{80,112},{96,64},{112,80},{1... | collective-permute-start | bytes 786440 | tf_op jit(solution)/shard_map/ppermute | solution.py:33
  127.7 8.4 %collective-permute-start.11 = (bf16[128,1024]{1,0:T(8,128)(2,1)S(1)}, bf16[128,1024]{1,0:T(8,128)(2,1)S(1)}, u32[]{:S(2)}, u32[]{:S(2)}) collective-permute-start(bf16[128,1024]{1,0:T(8,128)(2,1)S(1)} %get-tuple-element.13), channel_id=1, source_target_pairs={{0,32},{16,48},{32,0},{48,16},{64,96},{80,112},{96,64},{112,80},{1... | collective-permute-start | bytes 786440 | tf_op jit(solution)/shard_map/ppermute | solution.py:33
  136.2 21.0 %collective-permute-start.12 = (bf16[2,128,1024]{2,1,0:T(8,128)(2,1)S(1)}, bf16[2,128,1024]{2,1,0:T(8,128)(2,1)S(1)}, u32[]{:S(2)}, u32[]{:S(2)}) collective-permute-start(bf16[2,128,1024]{2,1,0:T(8,128)(2,1)S(1)} %bitcast_dynamic-update-slice_fusion.10), channel_id=1, source_target_pairs={{0,64},{16,80},{32,96},{48,112},{64,128},{80,144},{96,160},{112,17... | collective-permute-start | bytes 1572872 | tf_op jit(solution)/shard_map/ppermute | solution.py:33
  136.3 21.7 %collective-permute-start.13 = (bf16[2,128,1024]{2,1,0:T(8,128)(2,1)S(1)}, bf16[2,128,1024]{2,1,0:T(8,128)(2,1)S(1)}, u32[]{:S(2)}, u32[]{:S(2)}) collective-permute-start(bf16[2,128,1024]{2,1,0:T(8,128)(2,1)S(1)} %bitcast_dynamic-update-slice_fusion.10), channel_id=1, source_target_pairs={{0,192},{16,208},{32,224},{48,240},{64,0},{80,16},{96,32},{112,48}... | collective-permute-start | bytes 1572872 | tf_op jit(solution)/shard_map/ppermute | solution.py:33
  138.9 34.9 %collective-permute-start.14 = (bf16[2,128,1024]{2,1,0:T(8,128)(2,1)S(1)}, bf16[2,128,1024]{2,1,0:T(8,128)(2,1)S(1)}, u32[]{:S(2)}, u32[]{:S(2)}) collective-permute-start(bf16[2,128,1024]{2,1,0:T(8,128)(2,1)S(1)} %bitcast_dynamic-update-slice_fusion.10), channel_id=1, source_target_pairs={{0,128},{16,144},{32,160},{48,176},{64,192},{80,208},{96,224},{112... | collective-permute-start | bytes 1572872 | tf_op jit(solution)/shard_map/ppermute | solution.py:33
  174.6 7.3 %collective-permute-start.15 = (bf16[4,2,128,1024]{3,2,1,0:T(8,128)(2,1)}, bf16[4,2,128,1024]{3,2,1,0:T(8,128)(2,1)}, u32[]{:S(2)}, u32[]{:S(2)}) collective-permute-start(bf16[4,2,128,1024]{3,2,1,0:T(8,128)(2,1)} %bitcast_dynamic-update-slice_fusion.6), channel_id=1, source_target_pairs={{0,16},{16,0},{32,48},{48,32},{64,80},{80,64},{96,112},{112,96},{1... | collective-permute-start | bytes 6291464 | tf_op jit(solution)/shard_map/ppermute | solution.py:33
  180.3 3.6 %copy-start.7 = (bf16[768,1024]{1,0:T(8,128)(2,1)S(1)}, bf16[768,1024]{1,0:T(8,128)(2,1)}, u32[]{:S(2)}) copy-start(bf16[768,1024]{1,0:T(8,128)(2,1)} %param.8) | copy-start | bytes 4718596
  183.9 3.5 %copy-start.3 = (bf16[4,2,2,128,1024]{4,3,2,1,0:T(8,128)(2,1)}, bf16[4,2,2,128,1024]{4,3,2,1,0:T(8,128)(2,1)S(1)}, u32[]{:S(2)}) copy-start(bf16[4,2,2,128,1024]{4,3,2,1,0:T(8,128)(2,1)S(1)} %bitcast_dynamic-update-slice_fusion.1) | copy-start | bytes 12582916
  187.4 2.9 %copy-start.4 = (f32[4,4,128,768]{3,2,1,0:T(8,128)}, f32[4,4,128,768]{3,2,1,0:T(8,128)S(1)}, u32[]{:S(2)}) copy-start(f32[4,4,128,768]{3,2,1,0:T(8,128)S(1)} %fusion) | copy-start | bytes 18874372
  190.3 20.2 %collective-permute-start.16 = (bf16[4,128,768]{2,1,0:T(8,128)(2,1)}, bf16[4,128,768]{2,1,0:T(8,128)(2,1)S(1)}, u32[]{:S(2)}, u32[]{:S(2)}) collective-permute-start(bf16[4,128,768]{2,1,0:T(8,128)(2,1)} %get-tuple-element.14), channel_id=1, source_target_pairs={{0,1},{1,2},{2,3},{3,0},{4,5},{5,6},{6,7},{7,4},{8,9},{9,10},{10,1... | collective-permute-start | bytes 2359304 | tf_op jit(solution)/shard_map/ppermute | solution.py:33
  191.5 19.0 %collective-permute-start.17 = (bf16[4,128,768]{2,1,0:T(8,128)(2,1)S(1)}, bf16[4,128,768]{2,1,0:T(8,128)(2,1)S(1)}, u32[]{:S(2)}, u32[]{:S(2)}) collective-permute-start(bf16[4,128,768]{2,1,0:T(8,128)(2,1)S(1)} %get-tuple-element.16), channel_id=1, source_target_pairs={{0,3},{1,0},{2,1},{3,2},{4,7},{5,4},{6,5},{7,6},{8,11},{9,8},{10,9... | collective-permute-start | bytes 2359304 | tf_op jit(solution)/shard_map/ppermute | solution.py:33
  192.9 35.4 %collective-permute-start.18 = (bf16[4,128,768]{2,1,0:T(8,128)(2,1)S(1)}, bf16[4,128,768]{2,1,0:T(8,128)(2,1)}, u32[]{:S(2)}, u32[]{:S(2)}) collective-permute-start(bf16[4,128,768]{2,1,0:T(8,128)(2,1)S(1)} %get-tuple-element.15), channel_id=1, source_target_pairs={{0,2},{1,3},{2,0},{3,1},{4,6},{5,7},{6,4},{7,5},{8,10},{9,11},{10,... | collective-permute-start | bytes 2359304 | tf_op jit(solution)/shard_map/ppermute | solution.py:33
  230.4 17.9 %collective-permute-start.19 = (bf16[128,768]{1,0:T(8,128)(2,1)S(1)}, bf16[128,768]{1,0:T(8,128)(2,1)S(1)}, u32[]{:S(2)}, u32[]{:S(2)}) collective-permute-start(bf16[128,768]{1,0:T(8,128)(2,1)S(1)} %get-tuple-element.22), channel_id=1, source_target_pairs={{0,4},{1,5},{2,6},{3,7},{4,8},{5,9},{6,10},{7,11},{8,12},{9,13},{1... | collective-permute-start | bytes 589832 | tf_op jit(solution)/shard_map/ppermute | solution.py:33
  230.4 17.8 %collective-permute-start.20 = (bf16[128,768]{1,0:T(8,128)(2,1)S(1)}, bf16[128,768]{1,0:T(8,128)(2,1)S(1)}, u32[]{:S(2)}, u32[]{:S(2)}) collective-permute-start(bf16[128,768]{1,0:T(8,128)(2,1)S(1)} %get-tuple-element.24), channel_id=1, source_target_pairs={{0,12},{1,13},{2,14},{3,15},{4,0},{5,1},{6,2},{7,3},{8,4},{9,5},{1... | collective-permute-start | bytes 589832 | tf_op jit(solution)/shard_map/ppermute | solution.py:33
  234.0 14.5 %collective-permute-start.21 = (bf16[128,768]{1,0:T(8,128)(2,1)S(1)}, bf16[128,768]{1,0:T(8,128)(2,1)S(1)}, u32[]{:S(2)}, u32[]{:S(2)}) collective-permute-start(bf16[128,768]{1,0:T(8,128)(2,1)S(1)} %get-tuple-element.23), channel_id=1, source_target_pairs={{0,8},{1,9},{2,10},{3,11},{4,12},{5,13},{6,14},{7,15},{8,0},{9,1},... | collective-permute-start | bytes 589832 | tf_op jit(solution)/shard_map/ppermute | solution.py:33
  249.3 8.4 %copy-start.1 = (bf16[1024,768]{1,0:T(8,128)(2,1)S(1)}, bf16[1024,768]{1,0:T(8,128)(2,1)}, u32[]{:S(2)}) copy-start(bf16[1024,768]{1,0:T(8,128)(2,1)} %param.9) | copy-start | bytes 4718596
Sparse Core Ops, SparseCore 0:
  32.7 81.9 all-gather.2
  122.9 46.2 all-gather.4
